TPU v7x, 32 devices: a whole 2x2x4 slice. The times are simulated.
32 devices in a mesh: leaf: 8 (over z, x), sep: 4 (over y, core).
Axes of the slice: x: 2, y: 2, z: 4, core: 2. Of those that a mesh axis runs over, the one named last changes fastest.
Arguments:
- right_side: float32 [32768, 128], P(('leaf', 'sep')), may hold values from -6 to 6
- inverse_root: bfloat16 [8192, 8192], P(('leaf', 'sep')), may hold values from -1 to 3
- inverse_middle: bfloat16 [8192, 4096], P(('leaf', 'sep')), may hold values from -1 to 3
- inverse_lower: bfloat16 [16384, 4096], P(('leaf', 'sep')), may hold values from -1 to 3
- update_middle: bfloat16 [8192, 128], P(('leaf', 'sep')), may hold values from -0.09375 to 0.09375
- update_lower: bfloat16 [16384, 64], P(('leaf', 'sep')), may hold values from -0.09375 to 0.09375
- target_middle: int32 [32, 1], P(('leaf', 'sep')), may hold values from 0 to 31
- target_lower: int32 [32, 1], P(('leaf', 'sep')), may hold values from 0 to 63
Outputs:
- solution: float32 [32768, 128], P(('leaf', 'sep'))
All inputs are finite; a program needn't handle non-finite values.
Results may differ from a plain program's by a relative error of at most 0.0037.
Values may be sent and summed in bfloat16 or wider, within the bound.
A program may use at most 64 MiB of HBM per device.

v0:
```python
import jax
import jax.numpy as jnp
from jax import lax
from jax.sharding import PartitionSpec as P

BLOCK = 8


def from_partner(block, axis, distance):
    count = lax.axis_size(axis)
    route = []
    for low in range(count):
        high = low | 1 << distance
        if high != low and high < count:
            route += [(low, high), (high, low)]
    return lax.ppermute(block, axis, route)


def on_device(
    right_side,
    inverse_root,
    inverse_middle,
    inverse_lower,
    update_middle,
    update_lower,
    target_middle,
    target_lower,
):
    leaf_index = lax.axis_index("leaf")
    leaf_count = lax.axis_size("leaf")
    leaf_bits = leaf_count.bit_length() - 1
    dev_rows = inverse_root.shape[0]
    width = right_side.shape[1]
    root_side = right_side[:dev_rows]
    middle_side = right_side[dev_rows : 2 * dev_rows]
    lower_side = right_side[2 * dev_rows :]

    def collect(piece, depth_bits):
        panel = lax.all_gather(piece, "sep", axis=0, tiled=True)
        for bit_index in range(depth_bits):
            partner = from_partner(panel, "leaf", bit_index)
            upper = leaf_index >> bit_index & 1 == 1
            first = jnp.where(upper, partner, panel)
            second = jnp.where(upper, panel, partner)
            panel = jnp.concatenate([first, second], axis=0)
        return panel

    def apply_inverse(inverse, words, depth_bits):
        panel = collect(words, depth_bits)
        return jnp.dot(inverse, panel, preferred_element_type=jnp.float32)

    def halve_whole(current, depth_bits):
        for bit_index in reversed(range(depth_bits)):
            half = current.shape[0] // 2
            upper = leaf_index >> bit_index & 1 == 1
            keep = jnp.where(upper, current[half:], current[:half])
            give = jnp.where(upper, current[:half], current[half:])
            current = keep + from_partner(give, "leaf", bit_index)
        return current

    def reduce_slots(partial_value, depth_bits):
        current = halve_whole(partial_value, depth_bits)
        return lax.psum_scatter(current, "sep", scatter_dimension=0, tiled=True)

    def selector(targets, blocks):
        return (jnp.arange(blocks, dtype=jnp.int32)[:, None] == targets[0][None, :]).astype(
            jnp.float32
        )

    def place_slots(summed, targets, blocks):
        onehot = selector(targets, blocks)
        flat = summed.reshape(targets.shape[1], BLOCK * width)
        placed = jnp.dot(onehot, flat, precision=lax.Precision.HIGHEST)
        return placed.reshape(blocks * BLOCK, width)

    def pick_slots(table, targets, blocks):
        onehot = selector(targets, blocks)
        flat = table.astype(jnp.float32).reshape(blocks, BLOCK * width)
        picked = jnp.dot(onehot.T, flat, precision=lax.Precision.HIGHEST)
        return picked.reshape(targets.shape[1] * BLOCK, width).astype(jnp.bfloat16)

    contract_rows = (((0,), (0,)), ((), ()))
    lower_blocks = 2 * dev_rows // BLOCK
    middle_blocks = dev_rows // BLOCK
    lower_words = lower_side.astype(jnp.bfloat16)
    lower_values = apply_inverse(inverse_lower, lower_words, leaf_bits - 2)
    lower_partial = lax.dot_general(
        update_lower, lower_words, contract_rows, preferred_element_type=jnp.float32
    )
    lower_accum = place_slots(
        reduce_slots(lower_partial, leaf_bits - 2), target_lower, lower_blocks
    )
    middle_words = (middle_side - lower_accum[dev_rows:]).astype(jnp.bfloat16)
    middle_values = apply_inverse(inverse_middle, middle_words, leaf_bits - 1)
    middle_partial = lax.dot_general(
        update_middle, middle_words, contract_rows, preferred_element_type=jnp.float32
    )
    middle_accum = place_slots(
        reduce_slots(middle_partial, leaf_bits - 1), target_middle, middle_blocks
    )
    root_words = (root_side - (lower_accum[:dev_rows] + middle_accum)).astype(jnp.bfloat16)
    root_solution = apply_inverse(inverse_root, root_words, leaf_bits)
    root_rounded = root_solution.astype(jnp.bfloat16)
    middle_slots = collect(pick_slots(root_rounded, target_middle, middle_blocks), leaf_bits - 1)
    middle_solution = middle_values - jnp.dot(
        update_middle, middle_slots, preferred_element_type=jnp.float32
    )
    middle_rounded = middle_solution.astype(jnp.bfloat16)
    table = jnp.concatenate([root_rounded, middle_rounded], axis=0)
    lower_slots = collect(pick_slots(table, target_lower, lower_blocks), leaf_bits - 2)
    lower_solution = lower_values - jnp.dot(
        update_lower, lower_slots, preferred_element_type=jnp.float32
    )
    return jnp.concatenate([root_solution, middle_solution, lower_solution], axis=0)


def solution(mesh):
    in_specs = (
        P(("leaf", "sep"), None),
        P(("leaf", "sep"), None),
        P(("leaf", "sep"), None),
        P(("leaf", "sep"), None),
        P(("leaf", "sep"), None),
        P(("leaf", "sep"), None),
        P(("leaf", "sep"), None),
        P(("leaf", "sep"), None),
    )
    out_specs = P(("leaf", "sep"), None)
    return jax.shard_map(
        on_device, mesh=mesh, in_specs=in_specs, out_specs=out_specs, check_vma=False
    )
```

profile of v0, /device:TPU:0, one launch (start us, length us, event | category | flops | bytes accessed | tf_op | source)
XLA Modules:
  0.0 152.9 jit_solution(7578756123601498769)
XLA Ops:
  0.0 0.0 copy-start
  0.0 1.3 fusion.44
  1.3 3.0 %collective-permute-start = (f32[32,128]{1,0:T(8,128)S(1)}, f32[32,128]{1,0:T(8,128)S(1)}, u32[]{:S(2)}, u32[]{:S(2)}) collective-permute-start(f32[32,128]{1,0:T(8,128)S(1)} %slice_select_fusion.2), channel_id=1, source_target_pairs={{0,4},{4,0},{8,12},{12,8},{16,20},{20,16},{24,28},{28,24},{1,5},{5... | collective-permute-start | bytes 49160 | tf_op jit(solution)/shard_map/ppermute | solution.py:16
  5.0 1.2 dynamic-slice
  6.9 0.0 collective-permute-done
  6.9 10.7 %all-reduce = f32[32,128]{1,0:T(8,128)S(1)} all-reduce(f32[32,128]{1,0:T(8,128)S(1)} %select_add_fusion.2), channel_id=2, replica_groups=mesh['leaf'=8,'sep'=4] {'sep'}, use_global_device_ids=true, to_apply=%region_0.1.clone | all-reduce | flops 4096 | bytes 32768
  17.6 0.1 broadcast_multiply_fusion
  17.7 0.9 subtract_convert_fusion.1
  18.6 1.1 convolution_bitcast_fusion
  19.7 1.6 %collective-permute-start.1 = (f32[64,128]{1,0:T(8,128)S(1)}, f32[64,128]{1,0:T(8,128)S(1)}, u32[]{:S(2)}, u32[]{:S(2)}) collective-permute-start(f32[64,128]{1,0:T(8,128)S(1)} %slice_select_fusion), channel_id=1, source_target_pairs={{0,8},{8,0},{4,12},{12,4},{16,24},{24,16},{20,28},{28,20},{1,9},{9... | collective-permute-start | bytes 98312 | tf_op jit(solution)/shard_map/ppermute | solution.py:16
  22.0 1.7 %collective-permute-done.1 = f32[64,128]{1,0:T(8,128)S(1)} collective-permute-done((f32[64,128]{1,0:T(8,128)S(1)}, f32[64,128]{1,0:T(8,128)S(1)}, u32[]{:S(2)}, u32[]{:S(2)}) %collective-permute-start.1) | collective-permute-done | bytes 32800 | tf_op jit(solution)/shard_map/ppermute | solution.py:16
  23.7 0.7 collective-permute-start.2
  24.4 3.1 %collective-permute-done.2 = f32[32,128]{1,0:T(8,128)S(1)} collective-permute-done((f32[32,128]{1,0:T(8,128)S(1)}, f32[32,128]{1,0:T(8,128)S(1)}, u32[]{:S(2)}, u32[]{:S(2)}) %collective-permute-start.2) | collective-permute-done | bytes 16416 | tf_op jit(solution)/shard_map/ppermute | solution.py:16
  27.5 10.1 %all-reduce.1 = f32[32,128]{1,0:T(8,128)S(1)} all-reduce(f32[32,128]{1,0:T(8,128)S(1)} %select_add_fusion.1), channel_id=3, replica_groups=mesh['leaf'=8,'sep'=4] {'sep'}, use_global_device_ids=true, to_apply=%region_1.2.clone | all-reduce | flops 4096 | bytes 32768
  37.6 0.1 slice_add_fusion
  37.7 0.9 subtract_convert_fusion
  38.7 5.8 %all_gather.15 = bf16[1024,128]{1,0:T(8,128)(2,1)S(1)} all-gather(bf16[256,128]{1,0:T(8,128)(2,1)S(1)} %subtract_convert_fusion), channel_id=1, replica_groups=mesh['leaf'=8,'sep'=4] {'sep'}, dimensions={0}, use_global_device_ids=true | all-gather | bytes 327680 | tf_op jit(solution)/shard_map/all_gather | solution.py:39
  44.5 0.7 collective-permute-start.3
  45.1 7.9 %collective-permute-done.3 = bf16[1024,128]{1,0:T(8,128)(2,1)S(1)} collective-permute-done((bf16[1024,128]{1,0:T(8,128)(2,1)S(1)}, bf16[1024,128]{1,0:T(8,128)(2,1)S(1)}, u32[]{:S(2)}, u32[]{:S(2)}) %collective-permute-start.3) | collective-permute-done | bytes 262176 | tf_op jit(solution)/shard_map/ppermute | solution.py:16
  53.0 0.1 broadcast_select_fusion.11
  53.1 1.6 %collective-permute-start.4 = (bf16[2048,128]{1,0:T(8,128)(2,1)S(1)}, bf16[2048,128]{1,0:T(8,128)(2,1)S(1)}, u32[]{:S(2)}, u32[]{:S(2)}) collective-permute-start(bf16[2048,128]{1,0:T(8,128)(2,1)S(1)} %pad_maximum_fusion.1), channel_id=1, source_target_pairs={{0,8},{8,0},{4,12},{12,4},{16,24},{24,16},{20,28},{28,20},{1,9},{9... | collective-permute-start | bytes 1572872 | tf_op jit(solution)/shard_map/ppermute | solution.py:16
  54.8 11.8 %collective-permute-done.4 = bf16[2048,128]{1,0:T(8,128)(2,1)S(1)} collective-permute-done((bf16[2048,128]{1,0:T(8,128)(2,1)S(1)}, bf16[2048,128]{1,0:T(8,128)(2,1)S(1)}, u32[]{:S(2)}, u32[]{:S(2)}) %collective-permute-start.4) | collective-permute-done | bytes 524320 | tf_op jit(solution)/shard_map/ppermute | solution.py:16
  66.6 0.2 broadcast_select_fusion.7
  66.8 1.1 pad_maximum_fusion
  67.8 2.6 %collective-permute-start.5 = (bf16[4096,128]{1,0:T(8,128)(2,1)}, bf16[4096,128]{1,0:T(8,128)(2,1)}, u32[]{:S(2)}, u32[]{:S(2)}) collective-permute-start(bf16[4096,128]{1,0:T(8,128)(2,1)} %pad_maximum_fusion), channel_id=1, source_target_pairs={{0,16},{16,0},{4,20},{20,4},{8,24},{24,8},{12,28},{28,12},{1,17},{... | collective-permute-start | bytes 3145736 | tf_op jit(solution)/shard_map/ppermute | solution.py:16
  70.4 5.8 %all_gather.16 = bf16[1024,128]{1,0:T(8,128)(2,1)S(1)} all-gather(bf16[256,128]{1,0:T(8,128)(2,1)S(1)} %subtract_convert_fusion.1), channel_id=1, replica_groups=mesh['leaf'=8,'sep'=4] {'sep'}, dimensions={0}, use_global_device_ids=true | all-gather | bytes 327680 | tf_op jit(solution)/shard_map/all_gather | solution.py:39
  76.2 0.7 collective-permute-start.6
  76.9 1.0 slice.81
  77.8 0.0 copy-done.3
  77.9 7.0 %collective-permute-done.6 = bf16[1024,128]{1,0:T(8,128)(2,1)} collective-permute-done((bf16[1024,128]{1,0:T(8,128)(2,1)S(1)}, bf16[1024,128]{1,0:T(8,128)(2,1)}, u32[]{:S(2)}, u32[]{:S(2)}) %collective-permute-start.6) | collective-permute-done | bytes 262176 | tf_op jit(solution)/shard_map/ppermute | solution.py:16
  84.9 1.1 broadcast_select_fusion.9
  85.9 0.0 copy-start.1
  85.9 0.7 copy-done.1
  86.7 0.8 pad_maximum_fusion.2
  87.5 1.6 %collective-permute-start.7 = (bf16[2048,128]{1,0:T(8,128)(2,1)}, bf16[2048,128]{1,0:T(8,128)(2,1)}, u32[]{:S(2)}, u32[]{:S(2)}) collective-permute-start(bf16[2048,128]{1,0:T(8,128)(2,1)} %pad_maximum_fusion.2), channel_id=1, source_target_pairs={{0,8},{8,0},{4,12},{12,4},{16,24},{24,16},{20,28},{28,20},{1,9},{9... | collective-permute-start | bytes 1572872 | tf_op jit(solution)/shard_map/ppermute | solution.py:16
  89.1 26.3 %collective-permute-done.5 = bf16[4096,128]{1,0:T(8,128)(2,1)} collective-permute-done((bf16[4096,128]{1,0:T(8,128)(2,1)}, bf16[4096,128]{1,0:T(8,128)(2,1)}, u32[]{:S(2)}, u32[]{:S(2)}) %collective-permute-start.5) | collective-permute-done | bytes 1048608 | tf_op jit(solution)/shard_map/ppermute | solution.py:16
  115.3 1.6 %broadcast_select_fusion.1 = (bf16[4096,128]{1,0:T(8,128)(2,1)S(1)}, bf16[4096,128]{1,0:T(8,128)(2,1)S(1)}) fusion(bf16[4096,128]{1,0:T(8,128)(2,1)} %collective-permute-done.5, pred[]{:T(512)S(6)} %eq.94, bf16[2048,128]{1,0:T(8,128)(2,1)S(1)} %get-tuple-element.12, bf16[2048,128]{1,0:T(8,128)(2,1)S(1)} %get-tuple-element.11), kind=kLoop, calls=%fused_computation.18 | loop fusion | flops 3145728 | bytes 4194305 | tf_op jit(solution)/shard_map/jit(_where)/select_n | solution.py:43
  117.0 2.2 %fusion.42 = (bf16[256,128]{0,1:T(8,128)(2,1)S(1)}, f32[256,128]{0,1:T(8,128)}) fusion(bf16[256,8192]{1,0:T(8,128)(2,1)S(1)} %copy-done.7, bf16[4096,128]{1,0:T(8,128)(2,1)S(1)} %get-tuple-element.6, bf16[4096,128]{1,0:T(8,128)(2,1)S(1)} %get-tuple-element.5), kind=kOutput, calls=%fused_computation.82 | convolution fusion | flops 541097984 | bytes 6488064 | tf_op jit(solution)/shard_map/dot_general | solution.py:50
  119.2 0.1 copy.13
  119.3 0.1 fusion.18
  119.5 5.2 %all_gather.17 = bf16[32,128]{1,0:T(8,128)(2,1)S(1)} all-gather(bf16[8,128]{1,0:T(8,128)(2,1)S(1)} %convert_element_type.28), channel_id=1, replica_groups=mesh['leaf'=8,'sep'=4] {'sep'}, dimensions={0}, use_global_device_ids=true | all-gather | bytes 10240 | tf_op jit(solution)/shard_map/all_gather | solution.py:39
  124.6 0.7 collective-permute-start.8
  125.3 7.2 %all_gather.18 = bf16[2048,128]{1,0:T(8,128)(2,1)S(1)} all-gather(bf16[512,128]{1,0:T(8,128)(2,1)S(1)} %slice.81), channel_id=1, replica_groups=mesh['leaf'=8,'sep'=4] {'sep'}, dimensions={0}, use_global_device_ids=true | all-gather | bytes 655360 | tf_op jit(solution)/shard_map/all_gather | solution.py:39
  132.5 1.1 collective-permute-start.10
  133.6 0.0 collective-permute-done.8
  133.6 0.7 collective-permute-start.9
  134.3 0.0 collective-permute-done.7
  134.3 1.2 broadcast_select_fusion.5
  135.5 1.9 %collective-permute-done.9 = bf16[64,128]{1,0:T(8,128)(2,1)S(1)} collective-permute-done((bf16[64,128]{1,0:T(8,128)(2,1)S(1)}, bf16[64,128]{1,0:T(8,128)(2,1)S(1)}, u32[]{:S(2)}, u32[]{:S(2)}) %collective-permute-start.9) | collective-permute-done | bytes 16416 | tf_op jit(solution)/shard_map/ppermute | solution.py:16
  137.4 0.2 fusion.21
  137.6 0.9 fusion.43
  138.5 0.0 copy-start.5
  138.5 0.1 copy.14
  138.7 0.1 reshape.84
  138.7 0.1 fusion.15
  138.9 5.2 %all_gather.19 = bf16[32,128]{1,0:T(8,128)(2,1)S(1)} all-gather(bf16[8,128]{1,0:T(8,128)(2,1)S(1)} %convert_element_type.30), channel_id=1, replica_groups=mesh['leaf'=8,'sep'=4] {'sep'}, dimensions={0}, use_global_device_ids=true | all-gather | bytes 10240 | tf_op jit(solution)/shard_map/all_gather | solution.py:39
  144.0 0.9 collective-permute-start.11
  144.9 1.8 %collective-permute-done.10 = bf16[2048,128]{1,0:T(8,128)(2,1)} collective-permute-done((bf16[2048,128]{1,0:T(8,128)(2,1)S(1)}, bf16[2048,128]{1,0:T(8,128)(2,1)}, u32[]{:S(2)}, u32[]{:S(2)}) %collective-permute-start.10) | collective-permute-done | bytes 524320 | tf_op jit(solution)/shard_map/ppermute | solution.py:16
  146.8 1.1 broadcast_select_fusion.3
  147.9 0.0 collective-permute-done.11
  147.9 0.2 fusion.25
  148.1 3.8 %fusion.4 = f32[512,128]{0,1:T(8,128)S(1)} fusion(f32[128,512]{1,0:T(8,128)S(1)} %fusion.25, bf16[512,4096]{1,0:T(8,128)(2,1)} %param.11, bf16[2048,128]{1,0:T(8,128)(2,1)S(1)} %get-tuple-element.8, bf16[2048,128]{1,0:T(8,128)(2,1)S(1)} %get-tuple-element.7), kind=kOutput, calls=%fused_computation.5 | convolution fusion | flops 539033600 | bytes 5767168 | tf_op jit(solution)/shard_map/dot_general | solution.py:50
  151.9 0.0 copy-done.6
  152.0 1.0 copy.15
  (33 shorter events, 0.3 us)
Async XLA Ops:
  0.0 137.6 %copy-start = (bf16[256,4096]{1,0:T(8,128)(2,1)S(1)}, bf16[256,4096]{1,0:T(8,128)(2,1)}, u32[]{:S(2)}) copy-start(bf16[256,4096]{1,0:T(8,128)(2,1)} %param.10) | copy-start | bytes 6291460
  1.3 5.6 %collective-permute-start = (f32[32,128]{1,0:T(8,128)S(1)}, f32[32,128]{1,0:T(8,128)S(1)}, u32[]{:S(2)}, u32[]{:S(2)}) collective-permute-start(f32[32,128]{1,0:T(8,128)S(1)} %slice_select_fusion.2), channel_id=1, source_target_pairs={{0,4},{4,0},{8,12},{12,8},{16,20},{20,16},{24,28},{28,24},{1,5},{5... | collective-permute-start | bytes 49160 | tf_op jit(solution)/shard_map/ppermute | solution.py:16
  19.7 4.0 %collective-permute-start.1 = (f32[64,128]{1,0:T(8,128)S(1)}, f32[64,128]{1,0:T(8,128)S(1)}, u32[]{:S(2)}, u32[]{:S(2)}) collective-permute-start(f32[64,128]{1,0:T(8,128)S(1)} %slice_select_fusion), channel_id=1, source_target_pairs={{0,8},{8,0},{4,12},{12,4},{16,24},{24,16},{20,28},{28,20},{1,9},{9... | collective-permute-start | bytes 98312 | tf_op jit(solution)/shard_map/ppermute | solution.py:16
  23.7 3.8 %collective-permute-start.2 = (f32[32,128]{1,0:T(8,128)S(1)}, f32[32,128]{1,0:T(8,128)S(1)}, u32[]{:S(2)}, u32[]{:S(2)}) collective-permute-start(f32[32,128]{1,0:T(8,128)S(1)} %slice_select_fusion.1), channel_id=1, source_target_pairs={{0,4},{4,0},{8,12},{12,8},{16,20},{20,16},{24,28},{28,24},{1,5},{5... | collective-permute-start | bytes 49160 | tf_op jit(solution)/shard_map/ppermute | solution.py:16
  44.5 8.6 %collective-permute-start.3 = (bf16[1024,128]{1,0:T(8,128)(2,1)S(1)}, bf16[1024,128]{1,0:T(8,128)(2,1)S(1)}, u32[]{:S(2)}, u32[]{:S(2)}) collective-permute-start(bf16[1024,128]{1,0:T(8,128)(2,1)S(1)} %all_gather.15), channel_id=1, source_target_pairs={{0,4},{4,0},{8,12},{12,8},{16,20},{20,16},{24,28},{28,24},{1,5},{5... | collective-permute-start | bytes 786440 | tf_op jit(solution)/shard_map/ppermute | solution.py:16
  53.1 13.4 %collective-permute-start.4 = (bf16[2048,128]{1,0:T(8,128)(2,1)S(1)}, bf16[2048,128]{1,0:T(8,128)(2,1)S(1)}, u32[]{:S(2)}, u32[]{:S(2)}) collective-permute-start(bf16[2048,128]{1,0:T(8,128)(2,1)S(1)} %pad_maximum_fusion.1), channel_id=1, source_target_pairs={{0,8},{8,0},{4,12},{12,4},{16,24},{24,16},{20,28},{28,20},{1,9},{9... | collective-permute-start | bytes 1572872 | tf_op jit(solution)/shard_map/ppermute | solution.py:16
  67.8 47.5 %collective-permute-start.5 = (bf16[4096,128]{1,0:T(8,128)(2,1)}, bf16[4096,128]{1,0:T(8,128)(2,1)}, u32[]{:S(2)}, u32[]{:S(2)}) collective-permute-start(bf16[4096,128]{1,0:T(8,128)(2,1)} %pad_maximum_fusion), channel_id=1, source_target_pairs={{0,16},{16,0},{4,20},{20,4},{8,24},{24,8},{12,28},{28,12},{1,17},{... | collective-permute-start | bytes 3145736 | tf_op jit(solution)/shard_map/ppermute | solution.py:16
  76.2 1.6 %copy-start.3 = (bf16[1024,128]{1,0:T(8,128)(2,1)}, bf16[1024,128]{1,0:T(8,128)(2,1)S(1)}, u32[]{:S(2)}) copy-start(bf16[1024,128]{1,0:T(8,128)(2,1)S(1)} %all_gather.16) | copy-start | bytes 786436
  76.2 8.7 %collective-permute-start.6 = (bf16[1024,128]{1,0:T(8,128)(2,1)S(1)}, bf16[1024,128]{1,0:T(8,128)(2,1)}, u32[]{:S(2)}, u32[]{:S(2)}) collective-permute-start(bf16[1024,128]{1,0:T(8,128)(2,1)S(1)} %all_gather.16), channel_id=1, source_target_pairs={{0,4},{4,0},{8,12},{12,8},{16,20},{20,16},{24,28},{28,24},{1,5},{5... | collective-permute-start | bytes 786440 | tf_op jit(solution)/shard_map/ppermute | solution.py:16
  85.9 0.7 copy-start.1
  87.5 29.5 %copy-start.7 = (bf16[256,8192]{1,0:T(8,128)(2,1)S(1)}, bf16[256,8192]{1,0:T(8,128)(2,1)}, u32[]{:S(2)}) copy-start(bf16[256,8192]{1,0:T(8,128)(2,1)} %param.9) | copy-start | bytes 12582916
  87.5 46.8 %collective-permute-start.7 = (bf16[2048,128]{1,0:T(8,128)(2,1)}, bf16[2048,128]{1,0:T(8,128)(2,1)}, u32[]{:S(2)}, u32[]{:S(2)}) collective-permute-start(bf16[2048,128]{1,0:T(8,128)(2,1)} %pad_maximum_fusion.2), channel_id=1, source_target_pairs={{0,8},{8,0},{4,12},{12,4},{16,24},{24,16},{20,28},{28,20},{1,9},{9... | collective-permute-start | bytes 1572872 | tf_op jit(solution)/shard_map/ppermute | solution.py:16
  117.0 17.3 %copy-start.2 = (bf16[1024,128]{1,0:T(8,128)(2,1)S(1)}, bf16[1024,128]{1,0:T(8,128)(2,1)}, u32[]{:S(2)}) copy-start(bf16[1024,128]{1,0:T(8,128)(2,1)} %copy-done.1) | copy-start | bytes 786436
  119.2 18.3 %copy-start.4 = (bf16[256,128]{1,0:T(8,128)(2,1)S(1)}, bf16[256,128]{1,0:T(8,128)(2,1)}, u32[]{:S(2)}) copy-start(bf16[256,128]{1,0:T(8,128)(2,1)} %param.12) | copy-start | bytes 196612
  124.6 9.0 %collective-permute-start.8 = (bf16[32,128]{1,0:T(8,128)(2,1)S(1)}, bf16[32,128]{1,0:T(8,128)(2,1)S(1)}, u32[]{:S(2)}, u32[]{:S(2)}) collective-permute-start(bf16[32,128]{1,0:T(8,128)(2,1)S(1)} %all_gather.17), channel_id=1, source_target_pairs={{0,4},{4,0},{8,12},{12,8},{16,20},{20,16},{24,28},{28,24},{1,5},{5... | collective-permute-start | bytes 24584 | tf_op jit(solution)/shard_map/ppermute | solution.py:16
  132.5 14.3 %collective-permute-start.10 = (bf16[2048,128]{1,0:T(8,128)(2,1)S(1)}, bf16[2048,128]{1,0:T(8,128)(2,1)}, u32[]{:S(2)}, u32[]{:S(2)}) collective-permute-start(bf16[2048,128]{1,0:T(8,128)(2,1)S(1)} %all_gather.18), channel_id=1, source_target_pairs={{0,4},{4,0},{8,12},{12,8},{16,20},{20,16},{24,28},{28,24},{1,5},{5... | collective-permute-start | bytes 1572872 | tf_op jit(solution)/shard_map/ppermute | solution.py:16
  133.6 3.8 %collective-permute-start.9 = (bf16[64,128]{1,0:T(8,128)(2,1)S(1)}, bf16[64,128]{1,0:T(8,128)(2,1)S(1)}, u32[]{:S(2)}, u32[]{:S(2)}) collective-permute-start(bf16[64,128]{1,0:T(8,128)(2,1)S(1)} %pad_maximum_fusion.5), channel_id=1, source_target_pairs={{0,8},{8,0},{4,12},{12,4},{16,24},{24,16},{20,28},{28,20},{1,9},{9... | collective-permute-start | bytes 49160 | tf_op jit(solution)/shard_map/ppermute | solution.py:16
  138.5 9.4 %copy-start.5 = (bf16[512,64]{0,1:T(8,128)(2,1)S(1)}, bf16[512,64]{0,1:T(8,128)(2,1)}, u32[]{:S(2)}) copy-start(bf16[512,64]{0,1:T(8,128)(2,1)} %param.13) | copy-start | bytes 196612
  144.0 3.9 %collective-permute-start.11 = (bf16[32,128]{1,0:T(8,128)(2,1)S(1)}, bf16[32,128]{1,0:T(8,128)(2,1)S(1)}, u32[]{:S(2)}, u32[]{:S(2)}) collective-permute-start(bf16[32,128]{1,0:T(8,128)(2,1)S(1)} %all_gather.19), channel_id=1, source_target_pairs={{0,4},{4,0},{8,12},{12,8},{16,20},{20,16},{24,28},{28,24},{1,5},{5... | collective-permute-start | bytes 24584 | tf_op jit(solution)/shard_map/ppermute | solution.py:16
  148.1 3.8 %copy-start.6 = (f32[256,128]{0,1:T(8,128)S(1)}, f32[256,128]{0,1:T(8,128)}, u32[]{:S(2)}) copy-start(f32[256,128]{0,1:T(8,128)} %get-tuple-element.24) | copy-start | bytes 393220
where the time goes:
time: 154 us; the launch traced here: 153 us
  waiting for transfers between devices  61.5 us (40%)
  blocking collectives  49.8 us (32%)
  starting transfers between devices  15.8 us (10%)
  matrix products  9.76 us (6%)
  other arithmetic  9.43 us (6%)
  local copies, waits for them, and re-layouts  4.34 us (3%)
  between operations  2.28 us (1%)
    ppermute x12, waiting for transfers between devices, from_partner(): return lax.ppermute(block, axis, route)  61.5 us
    all_gather x5, blocking collectives, collect(): panel = lax.all_gather(piece, 'sep', axis=0, tiled=True)  29.1 us
    unnamed x2, blocking collectives  20.8 us
    ppermute x12, starting transfers between devices, from_partner(): return lax.ppermute(block, axis, route)  15.8 us
    dot_general x3, matrix products, apply_inverse(): return jnp.dot(inverse, panel, preferred_element_type=jnp.float32)  6.77 us
    select_n x9, other arithmetic, collect(): first = jnp.where(upper, partner, panel)  5.36 us
  transfers between devices with their start and end apart: 12, of which 8 were waited for; matrix products, arithmetic and copies ran while one was open for 8% of the time, Pallas kernels for 0%

commit v1 on v0

--- a/solution.py
+++ b/solution.py
@@ -36,7 +36,14 @@
     lower_side = right_side[2 * dev_rows :]
 
     def collect(piece, depth_bits):
-        panel = lax.all_gather(piece, "sep", axis=0, tiled=True)
+        ring = [piece]
+        for hop in range(3):
+            ring.append(lax.ppermute(ring[-1], "sep", [(dev, (dev + 1) % 4) for dev in range(4)]))
+        panel = jnp.roll(
+            jnp.concatenate(ring[::-1], axis=0),
+            (lax.axis_index("sep") + 1) * ring[0].shape[0],
+            axis=0,
+        )
         for bit_index in range(depth_bits):
             partner = from_partner(panel, "leaf", bit_index)
             upper = leaf_index >> bit_index & 1 == 1

time: 154 us -> 167 us (1.084)
  blocking collectives: 49.8 us -> 20.8 us
  waiting for transfers between devices: 61.5 us -> 86.9 us
  local copies, waits for them, and re-layouts: 4.34 us -> 16.4 us
  other arithmetic: 9.43 us -> 13 us
    ppermute x0 -> x15, waiting for transfers between devices: none -> 34 us  [collect(): lax.ppermute(ring[-1], 'sep', [(dev, (dev + 1) % 4) for dev in range(4)])]
    all_gather x5 -> x0, blocking collectives: 29.1 us -> none  [collect(): panel = lax.all_gather(piece, 'sep', axis=0, tiled=True)]
    unnamed x17 -> x26, local copies, waits for them, and re-layouts: 1.98 us -> 12.3 us
    ppermute x12, waiting for transfers between devices: 61.5 us -> 52.9 us  [from_partner(): return lax.ppermute(block, axis, route)]
    concatenate x0 -> x4, other arithmetic: none -> 6.34 us  [collect(): jnp.roll(jnp.concatenate(ring[::-1], axis=0), (lax.axis_index('sep') + 1)...]
    ppermute x0 -> x15, starting transfers between devices: none -> 3.07 us  [collect(): lax.ppermute(ring[-1], 'sep', [(dev, (dev + 1) % 4) for dev in range(4)])]
    ppermute x12, starting transfers between devices: 15.8 us -> 13.9 us  [from_partner(): return lax.ppermute(block, axis, route)]
  transfers between devices with their start and end apart: 12 -> 27, of which waited for: 8 -> 20; matrix products, arithmetic and copies ran while one was open for 8% -> 17% of each run, Pallas kernels for 0% -> 0%
where the time goes in v1:
time: 167 us
  waiting for transfers between devices  86.9 us (52%)
  blocking collectives  20.8 us (12%)
  starting transfers between devices  17 us (10%)
  local copies, waits for them, and re-layouts  16.4 us (10%)
  other arithmetic  13 us (8%)
  matrix products  10.4 us (6%)
  between operations  2.31 us (1%)
    ppermute x12, waiting for transfers between devices, from_partner(): return lax.ppermute(block, axis, route)  52.9 us
    ppermute x15, waiting for transfers between devices, collect(): lax.ppermute(ring[-1], 'sep', [(dev, (dev + 1) % 4) for dev in range(4)])  34 us
    unnamed x2, blocking collectives  20.8 us
    ppermute x12, starting transfers between devices, from_partner(): return lax.ppermute(block, axis, route)  13.9 us
    unnamed x26, local copies, waits for them, and re-layouts  12.3 us
    dot_general x3, matrix products, apply_inverse(): return jnp.dot(inverse, panel, preferred_element_type=jnp.float32)  7.43 us
    concatenate x4, other arithmetic, collect(): jnp.roll(jnp.concatenate(ring[::-1], axis=0), (lax.axis_index('sep') + 1)...  6.34 us
    select_n x9, other arithmetic, collect(): first = jnp.where(upper, partner, panel)  4.34 us
  transfers between devices with their start and end apart: 27, of which 20 were waited for; matrix products, arithmetic and copies ran while one was open for 17% of the time, Pallas kernels for 0%

profile of v1, /device:TPU:0, one launch (start us, length us, event | category | flops | bytes accessed | tf_op | source)
XLA Modules:
  0.0 166.7 jit_solution(15585101325983672496)
XLA Ops:
  0.0 1.3 fusion.72
  1.3 3.0 %collective-permute-start = (f32[32,128]{1,0:T(8,128)S(1)}, f32[32,128]{1,0:T(8,128)S(1)}, u32[]{:S(2)}, u32[]{:S(2)}) collective-permute-start(f32[32,128]{1,0:T(8,128)S(1)} %slice_select_fusion.2), channel_id=1, source_target_pairs={{0,4},{4,0},{8,12},{12,8},{16,20},{20,16},{24,28},{28,24},{1,5},{5... | collective-permute-start | bytes 49160 | tf_op jit(solution)/shard_map/ppermute | solution.py:16
  5.0 1.2 dynamic-slice
  6.9 10.7 %all-reduce = f32[32,128]{1,0:T(8,128)S(1)} all-reduce(f32[32,128]{1,0:T(8,128)S(1)} %select_add_fusion.2), channel_id=2, replica_groups=mesh['leaf'=8,'sep'=4] {'sep'}, use_global_device_ids=true, to_apply=%region_0.1.clone | all-reduce | flops 4096 | bytes 32768
  17.7 0.9 subtract_convert_fusion.1
  18.6 1.1 convolution_bitcast_fusion
  19.7 1.6 collective-permute-start.1
  22.0 1.7 %collective-permute-done.1 = f32[64,128]{1,0:T(8,128)S(1)} collective-permute-done((f32[64,128]{1,0:T(8,128)S(1)}, f32[64,128]{1,0:T(8,128)S(1)}, u32[]{:S(2)}, u32[]{:S(2)}) %collective-permute-start.1) | collective-permute-done | bytes 32800 | tf_op jit(solution)/shard_map/ppermute | solution.py:16
  23.7 0.7 collective-permute-start.2
  24.4 3.1 %collective-permute-done.2 = f32[32,128]{1,0:T(8,128)S(1)} collective-permute-done((f32[32,128]{1,0:T(8,128)S(1)}, f32[32,128]{1,0:T(8,128)S(1)}, u32[]{:S(2)}, u32[]{:S(2)}) %collective-permute-start.2) | collective-permute-done | bytes 16416 | tf_op jit(solution)/shard_map/ppermute | solution.py:16
  27.5 10.1 %all-reduce.1 = f32[32,128]{1,0:T(8,128)S(1)} all-reduce(f32[32,128]{1,0:T(8,128)S(1)} %select_add_fusion.1), channel_id=3, replica_groups=mesh['leaf'=8,'sep'=4] {'sep'}, use_global_device_ids=true, to_apply=%region_1.2.clone | all-reduce | flops 4096 | bytes 32768
  37.9 3.7 %collective-permute-done.3 = bf16[256,128]{1,0:T(8,128)(2,1)S(1)} collective-permute-done((bf16[256,128]{1,0:T(8,128)(2,1)S(1)}, bf16[256,128]{1,0:T(8,128)(2,1)S(1)}, u32[]{:S(2)}, u32[]{:S(2)}) %collective-permute-start.3) | collective-permute-done | bytes 65568 | tf_op jit(solution)/shard_map/ppermute | solution.py:41
  41.5 3.7 %collective-permute-done.4 = bf16[256,128]{1,0:T(8,128)(2,1)S(1)} collective-permute-done((bf16[256,128]{1,0:T(8,128)(2,1)S(1)}, bf16[256,128]{1,0:T(8,128)(2,1)S(1)}, u32[]{:S(2)}, u32[]{:S(2)}) %collective-permute-start.4) | collective-permute-done | bytes 65568 | tf_op jit(solution)/shard_map/ppermute | solution.py:41
  45.2 3.7 %collective-permute-done.5 = bf16[256,128]{1,0:T(8,128)(2,1)S(1)} collective-permute-done((bf16[256,128]{1,0:T(8,128)(2,1)S(1)}, bf16[256,128]{1,0:T(8,128)(2,1)S(1)}, u32[]{:S(2)}, u32[]{:S(2)}) %collective-permute-start.5) | collective-permute-done | bytes 65568 | tf_op jit(solution)/shard_map/ppermute | solution.py:41
  48.9 3.3 %fusion.25 = bf16[1024,128]{1,0:T(8,128)(2,1)S(1)} fusion(s32[]{:T(128)S(6)} %select_n.186, bf16[256,128]{1,0:T(8,128)(2,1)S(1)} %collective-permute-done.5, bf16[256,128]{1,0:T(8,128)(2,1)S(1)} %collective-permute-done.4, bf16[256,128]{1,0:T(8,128)(2,1)S(1)} %collective-permute-done.3, bf16[256,128]{1,0:T(8,128)(2,1)S(1)} %subtract_convert_fusion), kind=kLoop, calls=%fused_computation.54 | loop fusion | flops 2097152 | bytes 524292 | tf_op jit(solution)/shard_map/jit(_roll_dynamic)/concatenate | solution.py:42
  52.2 0.7 collective-permute-start.6
  52.8 6.4 %collective-permute-done.6 = bf16[1024,128]{1,0:T(8,128)(2,1)S(1)} collective-permute-done((bf16[1024,128]{1,0:T(8,128)(2,1)S(1)}, bf16[1024,128]{1,0:T(8,128)(2,1)S(1)}, u32[]{:S(2)}, u32[]{:S(2)}) %collective-permute-start.6) | collective-permute-done | bytes 262176 | tf_op jit(solution)/shard_map/ppermute | solution.py:16
  59.3 1.6 collective-permute-start.7
  61.1 1.1 collective-permute-start.9
  62.1 3.3 %collective-permute-done.19 = bf16[512,128]{1,0:T(8,128)(2,1)S(1)} collective-permute-done((bf16[512,128]{1,0:T(8,128)(2,1)S(1)}, bf16[512,128]{1,0:T(8,128)(2,1)S(1)}, u32[]{:S(2)}, u32[]{:S(2)}) %collective-permute-start.19) | collective-permute-done | bytes 131104 | tf_op jit(solution)/shard_map/ppermute | solution.py:41
  65.5 0.7 collective-permute-done.9
  66.2 0.4 collective-permute-start.10
  66.5 4.0 %collective-permute-done.10 = bf16[256,128]{1,0:T(8,128)(2,1)S(1)} collective-permute-done((bf16[256,128]{1,0:T(8,128)(2,1)S(1)}, bf16[256,128]{1,0:T(8,128)(2,1)S(1)}, u32[]{:S(2)}, u32[]{:S(2)}) %collective-permute-start.10) | collective-permute-done | bytes 65568 | tf_op jit(solution)/shard_map/ppermute | solution.py:41
  70.6 1.1 collective-permute-start.21
  71.6 0.2 broadcast_select_fusion.7
  71.9 1.1 pad_maximum_fusion
  72.9 2.6 %collective-permute-start.8 = (bf16[4096,128]{1,0:T(8,128)(2,1)}, bf16[4096,128]{1,0:T(8,128)(2,1)}, u32[]{:S(2)}, u32[]{:S(2)}) collective-permute-start(bf16[4096,128]{1,0:T(8,128)(2,1)} %pad_maximum_fusion), channel_id=1, source_target_pairs={{0,16},{16,0},{4,20},{20,4},{8,24},{24,8},{12,28},{28,12},{1,17},{... | collective-permute-start | bytes 3145736 | tf_op jit(solution)/shard_map/ppermute | solution.py:16
  75.5 3.0 %fusion.18 = bf16[1024,128]{1,0:T(8,128)(2,1)S(1)} fusion(s32[]{:T(128)S(6)} %select_n.186, bf16[256,128]{1,0:T(8,128)(2,1)} %collective-permute-done.11, bf16[256,128]{1,0:T(8,128)(2,1)} %copy-done.7, bf16[256,128]{1,0:T(8,128)(2,1)S(1)} %collective-permute-done.9, bf16[256,128]{1,0:T(8,128)(2,1)S(1)} %subtract_convert_fusion.1), kind=kLoop, calls=%fused_computation.47 | loop fusion | flops 2097152 | bytes 524292 | tf_op jit(solution)/shard_map/jit(_roll_dynamic)/concatenate | solution.py:42
  78.5 1.2 collective-permute-start.12
  79.7 1.6 constant_dynamic-update-slice_fusion.7
  81.3 1.6 constant_dynamic-update-slice_fusion.6
  82.9 1.6 constant_dynamic-update-slice_fusion.5
  84.4 1.6 constant_dynamic-update-slice_fusion.4
  86.1 1.6 constant_dynamic-update-slice_fusion.3
  87.6 1.6 constant_dynamic-update-slice_fusion.2
  89.2 1.5 constant_dynamic-update-slice_fusion.1
  90.8 30.9 %collective-permute-done.8 = bf16[4096,128]{1,0:T(8,128)(2,1)} collective-permute-done((bf16[4096,128]{1,0:T(8,128)(2,1)}, bf16[4096,128]{1,0:T(8,128)(2,1)}, u32[]{:S(2)}, u32[]{:S(2)}) %collective-permute-start.8) | collective-permute-done | bytes 1048608 | tf_op jit(solution)/shard_map/ppermute | solution.py:16
  121.6 1.6 broadcast_select_fusion.1
  123.3 2.2 %fusion.70 = (bf16[256,128]{0,1:T(8,128)(2,1)S(1)}, f32[256,128]{0,1:T(8,128)}) fusion(bf16[256,8192]{1,0:T(8,128)(2,1)S(1)} %copy-done.8, bf16[4096,128]{1,0:T(8,128)(2,1)S(1)} %get-tuple-element.8, bf16[4096,128]{1,0:T(8,128)(2,1)S(1)} %get-tuple-element.6), kind=kOutput, calls=%fused_computation.151 | convolution fusion | flops 541097984 | bytes 6488064 | tf_op jit(solution)/shard_map/dot_general | solution.py:57
  125.7 1.6 constant_dynamic-update-slice_fusion
  127.3 1.4 collective-permute-done.14
  128.7 1.0 broadcast_select_fusion.9
  129.7 2.0 %collective-permute-done.15 = bf16[8,128]{1,0:T(8,128)(2,1)S(1)} collective-permute-done((bf16[8,128]{1,0:T(8,128)(2,1)S(1)}, bf16[8,128]{1,0:T(8,128)(2,1)S(1)}, u32[]{:S(2)}, u32[]{:S(2)}) %collective-permute-start.15) | collective-permute-done | bytes 2080 | tf_op jit(solution)/shard_map/ppermute | solution.py:41
  131.9 2.9 %collective-permute-done.16 = bf16[8,128]{1,0:T(8,128)(2,1)S(1)} collective-permute-done((bf16[8,128]{1,0:T(8,128)(2,1)S(1)}, bf16[8,128]{1,0:T(8,128)(2,1)S(1)}, u32[]{:S(2)}, u32[]{:S(2)}) %collective-permute-start.16) | collective-permute-done | bytes 2080 | tf_op jit(solution)/shard_map/ppermute | solution.py:41
  134.8 0.7 collective-permute-start.17
  135.5 1.1 constant_dynamic-slice_fusion
  136.5 1.5 collective-permute-start.22
  138.0 0.6 collective-permute-done.17
  138.7 7.7 %collective-permute-done.13 = bf16[2048,128]{1,0:T(8,128)(2,1)S(1)} collective-permute-done((bf16[2048,128]{1,0:T(8,128)(2,1)S(1)}, bf16[2048,128]{1,0:T(8,128)(2,1)S(1)}, u32[]{:S(2)}, u32[]{:S(2)}) %collective-permute-start.13) | collective-permute-done | bytes 524320 | tf_op jit(solution)/shard_map/ppermute | solution.py:16
  146.4 0.2 broadcast_select_fusion.5
  146.6 0.1 collective-permute-done.18
  146.8 0.2 fusion.35
  147.0 1.5 fusion.71
  148.7 0.1 fusion.29
  148.9 0.4 collective-permute-start.23
  149.2 2.6 %collective-permute-done.23 = bf16[8,128]{1,0:T(8,128)(2,1)S(1)} collective-permute-done((bf16[8,128]{1,0:T(8,128)(2,1)S(1)}, bf16[8,128]{1,0:T(8,128)(2,1)S(1)}, u32[]{:S(2)}, u32[]{:S(2)}) %collective-permute-start.23) | collective-permute-done | bytes 2080 | tf_op jit(solution)/shard_map/ppermute | solution.py:41
  151.9 3.0 %collective-permute-done.24 = bf16[8,128]{1,0:T(8,128)(2,1)S(1)} collective-permute-done((bf16[8,128]{1,0:T(8,128)(2,1)S(1)}, bf16[8,128]{1,0:T(8,128)(2,1)S(1)}, u32[]{:S(2)}, u32[]{:S(2)}) %collective-permute-start.24) | collective-permute-done | bytes 2080 | tf_op jit(solution)/shard_map/ppermute | solution.py:41
  154.9 3.0 %collective-permute-done.25 = bf16[8,128]{1,0:T(8,128)(2,1)S(1)} collective-permute-done((bf16[8,128]{1,0:T(8,128)(2,1)S(1)}, bf16[8,128]{1,0:T(8,128)(2,1)S(1)}, u32[]{:S(2)}, u32[]{:S(2)}) %collective-permute-start.25) | collective-permute-done | bytes 2080 | tf_op jit(solution)/shard_map/ppermute | solution.py:41
  157.9 0.2 collective-permute-start.26
  158.1 1.2 broadcast_select_fusion.3
  159.4 2.3 %collective-permute-done.26 = bf16[32,128]{1,0:T(8,128)(2,1)S(1)} collective-permute-done((bf16[32,128]{1,0:T(8,128)(2,1)S(1)}, bf16[32,128]{1,0:T(8,128)(2,1)S(1)}, u32[]{:S(2)}, u32[]{:S(2)}) %collective-permute-start.26) | collective-permute-done | bytes 8224 | tf_op jit(solution)/shard_map/ppermute | solution.py:16
  161.7 0.2 fusion.39
  161.9 3.8 %fusion.4 = f32[512,128]{0,1:T(8,128)S(1)} fusion(f32[128,512]{1,0:T(8,128)S(1)} %fusion.39, bf16[512,4096]{1,0:T(8,128)(2,1)} %param.15, bf16[2048,128]{1,0:T(8,128)(2,1)S(1)} %get-tuple-element.10, bf16[2048,128]{1,0:T(8,128)(2,1)S(1)} %get-tuple-element.9), kind=kOutput, calls=%fused_computation.5 | convolution fusion | flops 539033600 | bytes 5767168 | tf_op jit(solution)/shard_map/dot_general | solution.py:57
  165.7 1.0 copy.15
  (73 shorter events, 1.4 us)
Async XLA Ops:
  0.0 147.0 %copy-start = (bf16[256,4096]{1,0:T(8,128)(2,1)S(1)}, bf16[256,4096]{1,0:T(8,128)(2,1)}, u32[]{:S(2)}) copy-start(bf16[256,4096]{1,0:T(8,128)(2,1)} %param.14) | copy-start | bytes 6291460
  0.0 37.7 %copy-start.1 = (f32[1024,128]{1,0:T(8,128)S(1)}, f32[1024,128]{1,0:T(8,128)}, u32[]{:S(2)}) copy-start(f32[1024,128]{1,0:T(8,128)} %param.12) | copy-start | bytes 1572868
  1.3 5.6 %collective-permute-start = (f32[32,128]{1,0:T(8,128)S(1)}, f32[32,128]{1,0:T(8,128)S(1)}, u32[]{:S(2)}, u32[]{:S(2)}) collective-permute-start(f32[32,128]{1,0:T(8,128)S(1)} %slice_select_fusion.2), channel_id=1, source_target_pairs={{0,4},{4,0},{8,12},{12,8},{16,20},{20,16},{24,28},{28,24},{1,5},{5... | collective-permute-start | bytes 49160 | tf_op jit(solution)/shard_map/ppermute | solution.py:16
  19.7 4.0 %collective-permute-start.1 = (f32[64,128]{1,0:T(8,128)S(1)}, f32[64,128]{1,0:T(8,128)S(1)}, u32[]{:S(2)}, u32[]{:S(2)}) collective-permute-start(f32[64,128]{1,0:T(8,128)S(1)} %slice_select_fusion), channel_id=1, source_target_pairs={{0,8},{8,0},{4,12},{12,4},{16,24},{24,16},{20,28},{28,20},{1,9},{9... | collective-permute-start | bytes 98312 | tf_op jit(solution)/shard_map/ppermute | solution.py:16
  23.7 3.8 %collective-permute-start.2 = (f32[32,128]{1,0:T(8,128)S(1)}, f32[32,128]{1,0:T(8,128)S(1)}, u32[]{:S(2)}, u32[]{:S(2)}) collective-permute-start(f32[32,128]{1,0:T(8,128)S(1)} %slice_select_fusion.1), channel_id=1, source_target_pairs={{0,4},{4,0},{8,12},{12,8},{16,20},{20,16},{24,28},{28,24},{1,5},{5... | collective-permute-start | bytes 49160 | tf_op jit(solution)/shard_map/ppermute | solution.py:16
  37.8 3.7 %collective-permute-start.3 = (bf16[256,128]{1,0:T(8,128)(2,1)S(1)}, bf16[256,128]{1,0:T(8,128)(2,1)S(1)}, u32[]{:S(2)}, u32[]{:S(2)}) collective-permute-start(bf16[256,128]{1,0:T(8,128)(2,1)S(1)} %subtract_convert_fusion), channel_id=1, source_target_pairs={{0,1},{1,2},{2,3},{3,0},{4,5},{5,6},{6,7},{7,4},{8,9},{9,10},{10,1... | collective-permute-start | bytes 196616 | tf_op jit(solution)/shard_map/ppermute | solution.py:41
  41.5 3.7 %collective-permute-start.4 = (bf16[256,128]{1,0:T(8,128)(2,1)S(1)}, bf16[256,128]{1,0:T(8,128)(2,1)S(1)}, u32[]{:S(2)}, u32[]{:S(2)}) collective-permute-start(bf16[256,128]{1,0:T(8,128)(2,1)S(1)} %collective-permute-done.3), channel_id=1, source_target_pairs={{0,1},{1,2},{2,3},{3,0},{4,5},{5,6},{6,7},{7,4},{8,9},{9,10},{10,1... | collective-permute-start | bytes 196616 | tf_op jit(solution)/shard_map/ppermute | solution.py:41
  45.2 3.7 %collective-permute-start.5 = (bf16[256,128]{1,0:T(8,128)(2,1)S(1)}, bf16[256,128]{1,0:T(8,128)(2,1)S(1)}, u32[]{:S(2)}, u32[]{:S(2)}) collective-permute-start(bf16[256,128]{1,0:T(8,128)(2,1)S(1)} %collective-permute-done.4), channel_id=1, source_target_pairs={{0,1},{1,2},{2,3},{3,0},{4,5},{5,6},{6,7},{7,4},{8,9},{9,10},{10,1... | collective-permute-start | bytes 196616 | tf_op jit(solution)/shard_map/ppermute | solution.py:41
  52.2 7.1 %collective-permute-start.6 = (bf16[1024,128]{1,0:T(8,128)(2,1)S(1)}, bf16[1024,128]{1,0:T(8,128)(2,1)S(1)}, u32[]{:S(2)}, u32[]{:S(2)}) collective-permute-start(bf16[1024,128]{1,0:T(8,128)(2,1)S(1)} %fusion.25), channel_id=1, source_target_pairs={{0,4},{4,0},{8,12},{12,8},{16,20},{20,16},{24,28},{28,24},{1,5},{5... | collective-permute-start | bytes 786440 | tf_op jit(solution)/shard_map/ppermute | solution.py:16
  59.3 12.3 %collective-permute-start.7 = (bf16[2048,128]{1,0:T(8,128)(2,1)S(1)}, bf16[2048,128]{1,0:T(8,128)(2,1)S(1)}, u32[]{:S(2)}, u32[]{:S(2)}) collective-permute-start(bf16[2048,128]{1,0:T(8,128)(2,1)S(1)} %pad_maximum_fusion.1), channel_id=1, source_target_pairs={{0,8},{8,0},{4,12},{12,4},{16,24},{24,16},{20,28},{28,20},{1,9},{9... | collective-permute-start | bytes 1572872 | tf_op jit(solution)/shard_map/ppermute | solution.py:16
  61.0 4.4 %collective-permute-start.19 = (bf16[512,128]{1,0:T(8,128)(2,1)S(1)}, bf16[512,128]{1,0:T(8,128)(2,1)S(1)}, u32[]{:S(2)}, u32[]{:S(2)}) collective-permute-start(bf16[512,128]{1,0:T(8,128)(2,1)S(1)} %slice.81), channel_id=1, source_target_pairs={{0,1},{1,2},{2,3},{3,0},{4,5},{5,6},{6,7},{7,4},{8,9},{9,10},{10,1... | collective-permute-start | bytes 393224 | tf_op jit(solution)/shard_map/ppermute | solution.py:41
  61.1 5.1 %collective-permute-start.9 = (bf16[256,128]{1,0:T(8,128)(2,1)S(1)}, bf16[256,128]{1,0:T(8,128)(2,1)S(1)}, u32[]{:S(2)}, u32[]{:S(2)}) collective-permute-start(bf16[256,128]{1,0:T(8,128)(2,1)S(1)} %subtract_convert_fusion.1), channel_id=1, source_target_pairs={{0,1},{1,2},{2,3},{3,0},{4,5},{5,6},{6,7},{7,4},{8,9},{9,10},{10,1... | collective-permute-start | bytes 196616 | tf_op jit(solution)/shard_map/ppermute | solution.py:41
  65.5 6.2 %copy-start.2 = (bf16[512,128]{1,0:T(8,128)(2,1)}, bf16[512,128]{1,0:T(8,128)(2,1)S(1)}, u32[]{:S(2)}) copy-start(bf16[512,128]{1,0:T(8,128)(2,1)S(1)} %collective-permute-done.19) | copy-start | bytes 393220
  65.5 5.1 %collective-permute-start.20 = (bf16[512,128]{1,0:T(8,128)(2,1)S(1)}, bf16[512,128]{1,0:T(8,128)(2,1)}, u32[]{:S(2)}, u32[]{:S(2)}) collective-permute-start(bf16[512,128]{1,0:T(8,128)(2,1)S(1)} %collective-permute-done.19), channel_id=1, source_target_pairs={{0,1},{1,2},{2,3},{3,0},{4,5},{5,6},{6,7},{7,4},{8,9},{9,10},{10,1... | collective-permute-start | bytes 393224 | tf_op jit(solution)/shard_map/ppermute | solution.py:41
  66.2 4.4 %collective-permute-start.10 = (bf16[256,128]{1,0:T(8,128)(2,1)S(1)}, bf16[256,128]{1,0:T(8,128)(2,1)S(1)}, u32[]{:S(2)}, u32[]{:S(2)}) collective-permute-start(bf16[256,128]{1,0:T(8,128)(2,1)S(1)} %collective-permute-done.9), channel_id=1, source_target_pairs={{0,1},{1,2},{2,3},{3,0},{4,5},{5,6},{6,7},{7,4},{8,9},{9,10},{10,1... | collective-permute-start | bytes 196616 | tf_op jit(solution)/shard_map/ppermute | solution.py:41
  70.5 2.4 %copy-start.7 = (bf16[256,128]{1,0:T(8,128)(2,1)}, bf16[256,128]{1,0:T(8,128)(2,1)S(1)}, u32[]{:S(2)}) copy-start(bf16[256,128]{1,0:T(8,128)(2,1)S(1)} %collective-permute-done.10) | copy-start | bytes 196612
  70.6 5.0 %collective-permute-start.11 = (bf16[256,128]{1,0:T(8,128)(2,1)S(1)}, bf16[256,128]{1,0:T(8,128)(2,1)}, u32[]{:S(2)}, u32[]{:S(2)}) collective-permute-start(bf16[256,128]{1,0:T(8,128)(2,1)S(1)} %collective-permute-done.10), channel_id=1, source_target_pairs={{0,1},{1,2},{2,3},{3,0},{4,5},{5,6},{6,7},{7,4},{8,9},{9,10},{10,1... | collective-permute-start | bytes 196616 | tf_op jit(solution)/shard_map/ppermute | solution.py:41
  70.6 9.2 %collective-permute-start.21 = (bf16[512,128]{1,0:T(8,128)(2,1)}, bf16[512,128]{1,0:T(8,128)(2,1)}, u32[]{:S(2)}, u32[]{:S(2)}) collective-permute-start(bf16[512,128]{1,0:T(8,128)(2,1)} %collective-permute-done.20), channel_id=1, source_target_pairs={{0,1},{1,2},{2,3},{3,0},{4,5},{5,6},{6,7},{7,4},{8,9},{9,10},{10,1... | collective-permute-start | bytes 393224 | tf_op jit(solution)/shard_map/ppermute | solution.py:41
  72.9 48.7 %collective-permute-start.8 = (bf16[4096,128]{1,0:T(8,128)(2,1)}, bf16[4096,128]{1,0:T(8,128)(2,1)}, u32[]{:S(2)}, u32[]{:S(2)}) collective-permute-start(bf16[4096,128]{1,0:T(8,128)(2,1)} %pad_maximum_fusion), channel_id=1, source_target_pairs={{0,16},{16,0},{4,20},{20,4},{8,24},{24,8},{12,28},{28,12},{1,17},{... | collective-permute-start | bytes 3145736 | tf_op jit(solution)/shard_map/ppermute | solution.py:16
  78.5 50.2 %collective-permute-start.12 = (bf16[1024,128]{1,0:T(8,128)(2,1)S(1)}, bf16[1024,128]{1,0:T(8,128)(2,1)}, u32[]{:S(2)}, u32[]{:S(2)}) collective-permute-start(bf16[1024,128]{1,0:T(8,128)(2,1)S(1)} %fusion.18), channel_id=1, source_target_pairs={{0,4},{4,0},{8,12},{12,8},{16,20},{20,16},{24,28},{28,24},{1,5},{5... | collective-permute-start | bytes 786440 | tf_op jit(solution)/shard_map/ppermute | solution.py:16
  90.7 32.5 %copy-start.8 = (bf16[256,8192]{1,0:T(8,128)(2,1)S(1)}, bf16[256,8192]{1,0:T(8,128)(2,1)}, u32[]{:S(2)}) copy-start(bf16[256,8192]{1,0:T(8,128)(2,1)} %param.13) | copy-start | bytes 12582916
  125.7 3.0 %collective-permute-start.14 = (bf16[8,128]{1,0:T(8,128)(2,1)S(1)}, bf16[8,128]{1,0:T(8,128)(2,1)S(1)}, u32[]{:S(2)}, u32[]{:S(2)}) collective-permute-start(bf16[8,128]{1,0:T(8,128)(2,1)S(1)} %convert_element_type.28), channel_id=1, source_target_pairs={{0,1},{1,2},{2,3},{3,0},{4,5},{5,6},{6,7},{7,4},{8,9},{9,10},{10,1... | collective-permute-start | bytes 6152 | tf_op jit(solution)/shard_map/ppermute | solution.py:41
  128.7 3.0 %collective-permute-start.15 = (bf16[8,128]{1,0:T(8,128)(2,1)S(1)}, bf16[8,128]{1,0:T(8,128)(2,1)S(1)}, u32[]{:S(2)}, u32[]{:S(2)}) collective-permute-start(bf16[8,128]{1,0:T(8,128)(2,1)S(1)} %collective-permute-done.14), channel_id=1, source_target_pairs={{0,1},{1,2},{2,3},{3,0},{4,5},{5,6},{6,7},{7,4},{8,9},{9,10},{10,1... | collective-permute-start | bytes 6152 | tf_op jit(solution)/shard_map/ppermute | solution.py:41
  131.7 3.0 %collective-permute-start.16 = (bf16[8,128]{1,0:T(8,128)(2,1)S(1)}, bf16[8,128]{1,0:T(8,128)(2,1)S(1)}, u32[]{:S(2)}, u32[]{:S(2)}) collective-permute-start(bf16[8,128]{1,0:T(8,128)(2,1)S(1)} %collective-permute-done.15), channel_id=1, source_target_pairs={{0,1},{1,2},{2,3},{3,0},{4,5},{5,6},{6,7},{7,4},{8,9},{9,10},{10,1... | collective-permute-start | bytes 6152 | tf_op jit(solution)/shard_map/ppermute | solution.py:41
  131.7 15.1 %copy-start.3 = (bf16[256,128]{1,0:T(8,128)(2,1)S(1)}, bf16[256,128]{1,0:T(8,128)(2,1)}, u32[]{:S(2)}) copy-start(bf16[256,128]{1,0:T(8,128)(2,1)} %param.16) | copy-start | bytes 196612
  131.8 14.7 %collective-permute-start.13 = (bf16[2048,128]{1,0:T(8,128)(2,1)S(1)}, bf16[2048,128]{1,0:T(8,128)(2,1)S(1)}, u32[]{:S(2)}, u32[]{:S(2)}) collective-permute-start(bf16[2048,128]{1,0:T(8,128)(2,1)S(1)} %pad_maximum_fusion.2), channel_id=1, source_target_pairs={{0,8},{8,0},{4,12},{12,4},{16,24},{24,16},{20,28},{28,20},{1,9},{9... | collective-permute-start | bytes 1572872 | tf_op jit(solution)/shard_map/ppermute | solution.py:16
  134.8 3.8 %collective-permute-start.17 = (bf16[32,128]{1,0:T(8,128)(2,1)S(1)}, bf16[32,128]{1,0:T(8,128)(2,1)S(1)}, u32[]{:S(2)}, u32[]{:S(2)}) collective-permute-start(bf16[32,128]{1,0:T(8,128)(2,1)S(1)} %fusion.53), channel_id=1, source_target_pairs={{0,4},{4,0},{8,12},{12,8},{16,20},{20,16},{24,28},{28,24},{1,5},{5... | collective-permute-start | bytes 24584 | tf_op jit(solution)/shard_map/ppermute | solution.py:16
  136.5 21.6 %collective-permute-start.22 = (bf16[2048,128]{1,0:T(8,128)(2,1)S(1)}, bf16[2048,128]{1,0:T(8,128)(2,1)S(1)}, u32[]{:S(2)}, u32[]{:S(2)}) collective-permute-start(bf16[2048,128]{1,0:T(8,128)(2,1)S(1)} %constant_dynamic-slice_fusion), channel_id=1, source_target_pairs={{0,4},{4,0},{8,12},{12,8},{16,20},{20,16},{24,28},{28,24},{1,5},{5... | collective-permute-start | bytes 1572872 | tf_op jit(solution)/shard_map/ppermute | solution.py:16
  138.6 8.2 %collective-permute-start.18 = (bf16[64,128]{1,0:T(8,128)(2,1)S(1)}, bf16[64,128]{1,0:T(8,128)(2,1)S(1)}, u32[]{:S(2)}, u32[]{:S(2)}) collective-permute-start(bf16[64,128]{1,0:T(8,128)(2,1)S(1)} %pad_maximum_fusion.5), channel_id=1, source_target_pairs={{0,8},{8,0},{4,12},{12,4},{16,24},{24,16},{20,28},{28,20},{1,9},{9... | collective-permute-start | bytes 49160 | tf_op jit(solution)/shard_map/ppermute | solution.py:16
  148.5 13.2 %copy-start.4 = (bf16[512,64]{0,1:T(8,128)(2,1)S(1)}, bf16[512,64]{0,1:T(8,128)(2,1)}, u32[]{:S(2)}) copy-start(bf16[512,64]{0,1:T(8,128)(2,1)} %param.17) | copy-start | bytes 196612
  148.9 3.0 %collective-permute-start.23 = (bf16[8,128]{1,0:T(8,128)(2,1)S(1)}, bf16[8,128]{1,0:T(8,128)(2,1)S(1)}, u32[]{:S(2)}, u32[]{:S(2)}) collective-permute-start(bf16[8,128]{1,0:T(8,128)(2,1)S(1)} %convert_element_type.30), channel_id=1, source_target_pairs={{0,1},{1,2},{2,3},{3,0},{4,5},{5,6},{6,7},{7,4},{8,9},{9,10},{10,1... | collective-permute-start | bytes 6152 | tf_op jit(solution)/shard_map/ppermute | solution.py:41
  151.9 3.0 %collective-permute-start.24 = (bf16[8,128]{1,0:T(8,128)(2,1)S(1)}, bf16[8,128]{1,0:T(8,128)(2,1)S(1)}, u32[]{:S(2)}, u32[]{:S(2)}) collective-permute-start(bf16[8,128]{1,0:T(8,128)(2,1)S(1)} %collective-permute-done.23), channel_id=1, source_target_pairs={{0,1},{1,2},{2,3},{3,0},{4,5},{5,6},{6,7},{7,4},{8,9},{9,10},{10,1... | collective-permute-start | bytes 6152 | tf_op jit(solution)/shard_map/ppermute | solution.py:41
  154.9 3.0 %collective-permute-start.25 = (bf16[8,128]{1,0:T(8,128)(2,1)S(1)}, bf16[8,128]{1,0:T(8,128)(2,1)S(1)}, u32[]{:S(2)}, u32[]{:S(2)}) collective-permute-start(bf16[8,128]{1,0:T(8,128)(2,1)S(1)} %collective-permute-done.24), channel_id=1, source_target_pairs={{0,1},{1,2},{2,3},{3,0},{4,5},{5,6},{6,7},{7,4},{8,9},{9,10},{10,1... | collective-permute-start | bytes 6152 | tf_op jit(solution)/shard_map/ppermute | solution.py:41
  157.9 3.7 %collective-permute-start.26 = (bf16[32,128]{1,0:T(8,128)(2,1)S(1)}, bf16[32,128]{1,0:T(8,128)(2,1)S(1)}, u32[]{:S(2)}, u32[]{:S(2)}) collective-permute-start(bf16[32,128]{1,0:T(8,128)(2,1)S(1)} %fusion.46), channel_id=1, source_target_pairs={{0,4},{4,0},{8,12},{12,8},{16,20},{20,16},{24,28},{28,24},{1,5},{5... | collective-permute-start | bytes 24584 | tf_op jit(solution)/shard_map/ppermute | solution.py:16
  161.9 3.8 %copy-start.5 = (f32[256,128]{0,1:T(8,128)S(1)}, f32[256,128]{0,1:T(8,128)}, u32[]{:S(2)}) copy-start(f32[256,128]{0,1:T(8,128)} %get-tuple-element.26) | copy-start | bytes 393220
  161.9 3.8 %copy-start.6 = (f32[256,128]{0,1:T(8,128)S(1)}, f32[256,128]{0,1:T(8,128)}, u32[]{:S(2)}) copy-start(f32[256,128]{0,1:T(8,128)} %get-tuple-element.28) | copy-start | bytes 393220
